TPU v7x, 768 devices: a whole 4x8x12 slice. The times are simulated.
768 devices in a mesh: dp: 48 (over z, y_hi, core), tensor: 16 (over y_lo, x).
Axes of the slice: x: 4, y: 8 (y_hi: 2, y_lo: 4; y = y_hi * 4 + y_lo), z: 12, core: 2. Of those that a mesh axis runs over, the one named last changes fastest.
Arguments:
- hidden: bfloat16 [6144, 14336], P('dp', 'tensor'), may hold values from -6 to 6
- down_weight: bfloat16 [4096, 14336], P(None, 'tensor'), may hold values from -0.046875 to 0.046875
- encoder: bfloat16 [4096, 768], P(None, 'dp'), may hold values from -0.09375 to 0.09375
- decoder: bfloat16 [768, 4096], P(None, 'tensor'), may hold values from -0.21875 to 0.21875
- cotangent: bfloat16 [6144, 4096], P('dp', 'tensor'), may hold values from -6 to 6
Outputs:
- output: bfloat16 [6144, 4096], P('dp', 'tensor')
- grad_hidden: bfloat16 [6144, 14336], P('dp', 'tensor')
- grad_decoder: float32 [768, 4096], P('dp', 'tensor')
All inputs are finite; a program needn't handle non-finite values.
Results may differ from a plain program's by a relative error of at most 0.0057.
Values may be sent and summed in bfloat16 or wider, within the bound.
A program may use at most 64 MiB of HBM per device.

v0:
```python
import jax
import jax.numpy as jnp
from jax import lax
from jax.sharding import PartitionSpec as P


def combine_latent(own_terms):
    share = lax.psum_scatter(own_terms, "tensor", scatter_dimension=1, tiled=True).astype(
        jnp.bfloat16
    )
    return lax.all_gather(share, "tensor", axis=1, tiled=True)


def per_device(hidden, down_weight, encoder, decoder, cotangent):
    full_code = lax.all_gather(encoder, "dp", axis=1, tiled=True)
    partial_value = lax.dot_general(
        hidden, down_weight, (((1,), (1,)), ((), ())), preferred_element_type=jnp.float32
    ).astype(jnp.bfloat16)
    own_terms = jnp.dot(partial_value, full_code, preferred_element_type=jnp.float32)
    shared = combine_latent(own_terms)
    output = jnp.dot(shared, decoder, preferred_element_type=jnp.float32).astype(jnp.bfloat16)
    all_tokens = hidden.shape[0] * lax.axis_size("dp")
    factor = 1.0 / float(all_tokens) ** 0.5
    grad_decoder = (
        lax.psum_scatter(
            lax.dot_general(
                shared, cotangent, (((0,), (0,)), ((), ())), preferred_element_type=jnp.float32
            ),
            "dp",
            scatter_dimension=0,
            tiled=True,
        )
        * factor
    )
    grad_terms = lax.dot_general(
        cotangent, decoder, (((1,), (1,)), ((), ())), preferred_element_type=jnp.float32
    )
    grad_latent = combine_latent(grad_terms)
    grad_partial = lax.dot_general(
        grad_latent, full_code, (((1,), (1,)), ((), ())), preferred_element_type=jnp.float32
    ).astype(jnp.bfloat16)
    grad_hidden = jnp.dot(grad_partial, down_weight, preferred_element_type=jnp.float32).astype(
        jnp.bfloat16
    )
    return (output, grad_hidden, grad_decoder)


def solution(mesh):
    in_specs = (
        P("dp", "tensor"),
        P(None, "tensor"),
        P(None, "dp"),
        P(None, "tensor"),
        P("dp", "tensor"),
    )
    out_specs = (P("dp", "tensor"), P("dp", "tensor"), P("dp", "tensor"))
    return jax.shard_map(
        per_device, mesh=mesh, in_specs=in_specs, out_specs=out_specs, check_vma=False
    )
```

profile of v0, /device:TPU:6, one launch (start us, length us, event | category | flops | bytes accessed | tf_op | source)
XLA Modules:
  0.0 538.1 jit_solution(11019852469111814424)
XLA Ops:
  7.2 0.0 copy-start
  7.2 0.0 all-gather.2.cloned.1.call-start
  7.2 0.7 all-gather.2.cloned.1.call-update
  7.9 0.0 copy-start.1
  7.9 0.0 reduce-scatter.6.cloned.1.call-start
  8.0 159.0 %all-gather.2.cloned.1.call-done = bf16[4096,768]{0,1:T(8,128)(2,1)} async-done(((bf16[4096,16]{0,1:T(8,128)(2,1)}), bf16[4096,768]{0,1:T(8,128)(2,1)}) %all-gather.2.cloned.1.call-update) | async-done | bytes 6291472 | tf_op jit(solution)/shard_map/all_gather | solution.py:15
  166.9 9.8 %fusion = f32[128,768]{0,1:T(8,128)} fusion(bf16[4096,768]{0,1:T(8,128)(2,1)} %all-gather.2.cloned.1.call-done, bf16[128,896]{1,0:T(8,128)(2,1)} %param.5, bf16[4096,896]{1,0:T(8,128)(2,1)} %param.6), kind=kOutput, calls=%fused_computation.5 | convolution fusion | flops 1745354752 | bytes 14254080 | tf_op jit(solution)/shard_map/dot_general | solution.py:19
  176.7 0.0 reduce-scatter.6.cloned.1.call-update
  176.8 0.0 reduce-scatter.10.cloned.1.call-start
  176.8 0.0 copy-done
  176.8 0.0 copy-done.1
  176.8 1.0 convolution_bitcast_fusion
  177.8 0.0 reduce-scatter.10.cloned.1.call-update
  177.9 0.0 reduce-scatter.8.cloned.1.call-start
  177.9 78.5 %reduce-scatter.6.cloned.1.call-done = f32[128,48]{0,1:T(8,128)} async-done(((f32[128,768]{0,1:T(8,128)}), f32[128,48]{0,1:T(8,128)}) %reduce-scatter.6.cloned.1.call-update) | async-done | bytes 24592 | tf_op jit(solution)/shard_map/reduce_scatter | solution.py:8
  256.4 0.7 convert_element_type.19
  257.1 41.5 %all_gather.10 = bf16[128,768]{0,1:T(8,128)(2,1)S(1)} all-gather(bf16[128,48]{0,1:T(8,128)(2,1)S(1)} %convert_element_type.19), channel_id=1, replica_groups=mesh['dp'=48,'tensor'=16] {'tensor'}, dimensions={1}, use_global_device_ids=true | all-gather | bytes 208896 | tf_op jit(solution)/shard_map/all_gather | solution.py:11
  298.6 1.1 fusion.1
  299.8 0.0 reduce-scatter.8.cloned.1.call-update
  299.8 45.7 %reduce-scatter.10.cloned.1.call-done = f32[48,128]{1,0:T(8,128)} async-done(((f32[768,128]{1,0:T(8,128)}), f32[48,128]{1,0:T(8,128)}) %reduce-scatter.10.cloned.1.call-update) | async-done | bytes 24592
  345.5 0.7 bitcast_convert_fusion
  346.2 41.5 %all_gather.11 = bf16[128,768]{0,1:T(8,128)(2,1)S(1)} all-gather(bf16[128,48]{0,1:T(8,128)(2,1)S(1)} %bitcast_convert_fusion), channel_id=1, replica_groups=mesh['dp'=48,'tensor'=16] {'tensor'}, dimensions={1}, use_global_device_ids=true | all-gather | bytes 208896 | tf_op jit(solution)/shard_map/all_gather | solution.py:11
  387.6 7.8 %convolution_convert_fusion.2 = bf16[128,896]{1,0:T(8,128)(2,1)} fusion(bf16[4096,896]{1,0:T(8,128)(2,1)} %param.6, bf16[128,768]{0,1:T(8,128)(2,1)S(1)} %all_gather.11, bf16[4096,768]{0,1:T(8,128)(2,1)} %all-gather.2.cloned.1.call-done), kind=kOutput, calls=%fused_computation.3 | convolution fusion | flops 1745469440 | bytes 14057472 | tf_op jit(solution)/shard_map/dot_general | solution.py:42
  395.4 0.9 convolution_convert_fusion.3
  396.3 133.9 %reduce-scatter.8.cloned.1.call-done = f32[16,256]{1,0:T(8,128)} async-done(((f32[768,256]{1,0:T(8,128)}), f32[16,256]{1,0:T(8,128)}) %reduce-scatter.8.cloned.1.call-update) | async-done | bytes 16400 | tf_op jit(solution)/shard_map/reduce_scatter | solution.py:25
  530.2 1.3 broadcast_multiply_fusion
Async XLA Ops:
  7.2 169.6 %copy-start = (bf16[768,256]{1,0:T(8,128)(2,1)S(1)}, bf16[768,256]{1,0:T(8,128)(2,1)}, u32[]{:S(2)}) copy-start(bf16[768,256]{1,0:T(8,128)(2,1)} %param.8) | copy-start | bytes 1179652
  7.2 159.8 %all-gather.2.cloned.1.call-start = ((), (), s32[]{:S(2)}) async-start(), calls=%async_computation.3 | async-start | bytes 6422528 | tf_op jit(solution)/shard_map/all_gather | solution.py:15
  7.9 168.9 %copy-start.1 = (bf16[128,256]{1,0:T(8,128)(2,1)S(1)}, bf16[128,256]{1,0:T(8,128)(2,1)}, u32[]{:S(2)}) copy-start(bf16[128,256]{1,0:T(8,128)(2,1)} %param.9) | copy-start | bytes 196612
  7.9 248.4 %reduce-scatter.6.cloned.1.call-start = ((), (), s32[]{:S(2)}) async-start(), calls=%async_computation.4 | async-start | bytes 417792 | tf_op jit(solution)/shard_map/reduce_scatter | solution.py:8
  176.8 168.7 %reduce-scatter.10.cloned.1.call-start = ((), (), s32[]{:S(2)}) async-start(), calls=%async_computation.6 | async-start | bytes 417792
  177.9 352.4 %reduce-scatter.8.cloned.1.call-start = ((), (), s32[]{:S(2)}) async-start(), calls=%async_computation.5 | async-start | bytes 802816 | tf_op jit(solution)/shard_map/reduce_scatter | solution.py:25
Sparse Core Ops, SparseCore 0:
  11.7 155.2 all-gather.1
  176.9 79.4 reduce-scatter.5
  259.8 85.6 reduce-scatter.9
  350.5 179.6 reduce-scatter.7
where the time goes:
time: 538 us
  waiting for transfers between devices  418 us (78%)
  blocking collectives  83 us (15%)
  matrix products  20.6 us (4%)
  between operations  13.8 us (3%)
    all_gather x1, waiting for transfers between devices, per_device(): full_code = lax.all_gather(encoder, 'dp', axis=1, tiled=True)  159 us
    reduce_scatter x1, waiting for transfers between devices, per_device(): lax.psum_scatter(lax.dot_general(shared, cotangent, (((0,), (0,)), ((), (...  134 us
    all_gather x2, blocking collectives, combine_latent(): return lax.all_gather(share, 'tensor', axis=1, tiled=True)  83 us
    reduce_scatter x1, waiting for transfers between devices, combine_latent(): lax.psum_scatter(own_terms, 'tensor', scatter_dimension=1, tiled=True)  78.5 us
    unnamed x5, waiting for transfers between devices  46.4 us
  transfers between devices with their start and end apart: 4, of which 4 were waited for; matrix products, arithmetic and copies ran while one was open for 2% of the time, Pallas kernels for 0%

commit v1 on v0

v1 whole, which is shorter than its diff:
```python
import jax
import jax.numpy as jnp
from jax import lax
from jax.experimental import pallas as pl
from jax.experimental.pallas import tpu as pltpu
from jax.sharding import PartitionSpec as P

MESH = pl.DeviceIdType.MESH
F32, BF16 = jnp.float32, jnp.bfloat16
NZ, NT = 12, 16
NP = 2 * NZ
ROWS = 48
HUBS = (3, NZ - 3, 6)
CHUNKS = 8


def nt(a, b):
    return lax.dot_general(a, b, (((1,), (1,)), ((), ())), preferred_element_type=F32)


def nn(a, b):
    return jnp.dot(a, b, preferred_element_type=F32)


def tn(a, b):
    return lax.dot_general(a, b, (((0,), (0,)), ((), ())), preferred_element_type=F32)


def kernel(
    h_hbm, dw_hbm, enc_hbm, dec_hbm, cot_hbm,
    out_ref, gh_ref, gd_ref,
    dwv, encv, decv, cotv, hv, mv,
    gterm, gslot, gfull, gsib,
    sterm, sslot, sfull, ssib,
    dterm, dslot,
    lsem, wsem, msend, mrecv, psend, precv, asend, arecv,
):
    dp, t = lax.axis_index("dp"), lax.axis_index("tensor")
    z, yh, c = dp // 4, (dp // 2) % 2, dp % 2
    place = z * 2 + yh

    def device(zz, yy):
        return ((zz * 2 + yy) * 2 + c, t)

    sibling = (dp + 1 - 2 * c, t)

    def along(k):
        return lax.rem(z + (k % NZ), NZ)

    depth = dw_hbm.shape[0] // CHUNKS
    own = [
        pltpu.make_async_copy(enc_hbm, encv, lsem.at[0]),
        pltpu.make_async_copy(cot_hbm, cotv.at[c], lsem.at[1]),
        pltpu.make_async_copy(h_hbm, hv.at[c], lsem.at[2]),
        pltpu.make_async_copy(dec_hbm.at[:, 0], decv.at[0], lsem.at[3]),
        pltpu.make_async_copy(dec_hbm.at[:, 1], decv.at[1], lsem.at[4]),
    ]
    weights = [
        pltpu.make_async_copy(
            dw_hbm.at[pl.ds(i * depth, depth)], dwv.at[pl.ds(i * depth, depth)], wsem.at[i]
        )
        for i in range(CHUNKS)
    ]
    own[0].start()
    for copy in weights[:2]:
        copy.start()
    for copy in own[1:]:
        copy.start()
    for copy in weights[2:]:
        copy.start()

    barrier = pltpu.get_barrier_semaphore()
    greet = [sibling, device(z, 1 - yh), device(along(1), yh), device(along(-1), yh)]
    greet += [device(along(k), yh) for k in HUBS]
    for who in greet:
        pl.semaphore_signal(barrier, inc=1, device_id=who, device_id_type=MESH)

    @pl.loop(1, NT)
    def _(k):
        pl.semaphore_signal(
            barrier, inc=1, device_id=(dp, lax.rem(t + k, NT)), device_id_type=MESH
        )

    own[0].wait()
    code = jnp.zeros((16, dwv.shape[1]), F32)
    for i in range(CHUNKS):
        cut = pl.ds(i * depth, depth)
        weights[i].wait()
        code += nn(encv[:, cut], dwv[cut, :])
    mv[c, place] = code.astype(BF16)
    for copy in own[1:]:
        copy.wait()

    pl.semaphore_wait(barrier, len(greet) + NT - 1)

    sent = []

    def pass_on(zz, yy, to):
        slot = zz * 2 + yy
        copy = pltpu.make_async_remote_copy(
            src_ref=mv.at[c, slot],
            dst_ref=mv.at[c, slot],
            send_sem=msend.at[len(sent)],
            recv_sem=mrecv.at[slot],
            device_id=to,
            device_id_type=MESH,
        )
        copy.start()
        sent.append(copy)

    def arrived(zz, yy):
        slot = zz * 2 + yy
        pltpu.make_async_copy(mv.at[c, slot], mv.at[c, slot], mrecv.at[slot]).wait()

    def pass_near(zz, yy):
        pass_on(zz, yy, device(along(1), yh))
        pass_on(zz, yy, device(along(-1), yh))

    pairs = []

    def to_sibling(src, dst):
        i = len(pairs)
        copy = pltpu.make_async_remote_copy(
            src_ref=src, dst_ref=dst, send_sem=psend.at[i], recv_sem=precv.at[i],
            device_id=sibling, device_id_type=MESH,
        )
        copy.start()
        pairs.append(copy)
        return copy

    def scatter(term, slots, i):
        @pl.loop(1, NT)
        def _(k):
            who = lax.rem(t + k, NT)
            pltpu.make_async_remote_copy(
                src_ref=term.at[who], dst_ref=slots.at[k - 1],
                send_sem=asend.at[i], recv_sem=arecv.at[i],
                device_id=(dp, who), device_id_type=MESH,
            ).start()

    def gather(full, i):
        @pl.loop(1, NT)
        def _(k):
            pltpu.make_async_remote_copy(
                src_ref=full.at[t], dst_ref=full.at[t],
                send_sem=asend.at[i], recv_sem=arecv.at[i],
                device_id=(dp, lax.rem(t + k, NT)), device_id_type=MESH,
            ).start()

    def all_of(ref, sem):
        pltpu.make_async_copy(ref, ref, sem).wait()

    def summed(term, slots):
        total = term[t].astype(F32)
        for k in range(NT - 1):
            total += slots[k].astype(F32)
        return total.astype(BF16)

    def split(term, value):
        for r in range(NT // 2):
            for s in range(2):
                term[2 * r + s] = value[r * ROWS:(r + 1) * ROWS, s * 128:(s + 1) * 128].astype(BF16)

    for k in HUBS:
        pass_on(z, yh, device(along(k), yh))
    pass_on(z, yh, device(z, 1 - yh))
    pass_near(z, yh)
    cot_pair = to_sibling(cotv.at[c], cotv.at[c])
    hid_pair = to_sibling(hv.at[c], hv.at[c])

    cot_pair.wait_recv()
    cot_both = cotv[...].reshape(-1, cotv.shape[2])
    split(gterm, nt(decv[c].reshape(-1, decv.shape[3]), cot_both))
    scatter(gterm, gslot, 0)

    arrived(z, 1 - yh)
    pass_near(z, 1 - yh)
    for k in HUBS:
        arrived(along(k), yh)
        pass_on(along(k), yh, device(z, 1 - yh))
        pass_near(along(k), yh)

    all_of(gslot, arecv.at[0])
    gfull[t] = summed(gterm, gslot)
    gather(gfull, 1)

    for k in HUBS:
        arrived(along(k), 1 - yh)
        pass_near(along(k), 1 - yh)
    for side in (1, -1):
        for k in (0,) + HUBS:
            for yy in range(2):
                arrived(along(side + k), yy)

    m_pair = to_sibling(mv.at[c], mv.at[c])
    hid_pair.wait_recv()
    width = hv.shape[2]
    split(sterm, nt(mv[c].reshape(-1, width), hv[...].reshape(-1, width)))
    scatter(sterm, sslot, 2)

    def own_tokens(full):
        return jnp.concatenate([full[2 * r + c] for r in range(NT // 2)], axis=0)

    def swap(full, sib):
        copies = []
        for r in range(NT // 2):
            copies.append(to_sibling(full.at[2 * r + 1 - c], sib.at[r]))
        return copies

    all_of(gfull.at[pl.ds(0, NT - 1)], arecv.at[1])
    g_swap = swap(gfull, gsib)
    m_pair.wait_recv()
    for copy in g_swap:
        copy.wait_recv()
    gh = tn(own_tokens(gfull), mv[c].reshape(-1, width))
    gh += tn(gsib[...].reshape(-1, 128), mv[1 - c].reshape(-1, width))
    gh_ref[...] = gh.astype(BF16)

    all_of(sslot, arecv.at[2])
    sfull[t] = summed(sterm, sslot)
    gather(sfull, 3)
    all_of(sfull.at[pl.ds(0, NT - 1)], arecv.at[3])

    left = jnp.concatenate([sfull[2 * r] for r in range(NT // 2)], axis=0)
    right = jnp.concatenate([sfull[2 * r + 1] for r in range(NT // 2)], axis=0)
    gd = nn(left, cotv[0]) + nn(right, cotv[1])
    dterm[...] = gd.astype(BF16).reshape(dterm.shape)

    @pl.loop(1, NP)
    def _(k):
        who = lax.rem(place + k, NP)
        pltpu.make_async_remote_copy(
            src_ref=dterm.at[who], dst_ref=dslot.at[k - 1],
            send_sem=asend.at[4], recv_sem=arecv.at[4],
            device_id=(who * 2 + c, t), device_id_type=MESH,
        ).start()

    s_swap = swap(sfull, ssib)
    for copy in s_swap:
        copy.wait_recv()
    value = tn(own_tokens(sfull), decv[c].reshape(-1, decv.shape[3]))
    value += tn(ssib[...].reshape(-1, 128), decv[1 - c].reshape(-1, decv.shape[3]))
    out_ref[...] = value.astype(BF16)

    all_of(dslot, arecv.at[4])
    total = dterm[place].astype(F32)
    for k in range(NP - 1):
        total += dslot[k].astype(F32)
    gd_ref[...] = total * (1.0 / 6144.0**0.5)

    for copy in sent:
        copy.wait_send()
    for copy in pairs:
        copy.wait_send()
    for i, ref in enumerate((gslot, gslot, gslot, gslot, dslot)):
        all_of(ref, asend.at[i])


def write_out(a, b, c, a_out, b_out, c_out, sem):
    copies = [
        pltpu.make_async_copy(src, dst, sem.at[i])
        for i, (src, dst) in enumerate(((a, a_out), (b, b_out), (c, c_out)))
    ]
    for copy in copies:
        copy.start()
    for copy in copies:
        copy.wait()


def per_device(hidden, down_weight, encoder, decoder, cotangent):
    tokens, width = hidden.shape
    model = down_weight.shape[0]
    wide = decoder.shape[1]
    hbm = pl.BlockSpec(memory_space=pltpu.HBM)
    vmem = pl.BlockSpec(memory_space=pltpu.VMEM)
    V, D = pltpu.VMEM, pltpu.SemaphoreType.DMA

    def exchange():
        return [
            V((NT, ROWS, 128), BF16),
            V((NT - 1, ROWS, 128), BF16),
            V((NT, ROWS, 128), BF16),
            V((NT // 2, ROWS, 128), BF16),
        ]

    results = pl.pallas_call(
        kernel,
        out_shape=(
            jax.ShapeDtypeStruct((tokens, wide), BF16),
            jax.ShapeDtypeStruct((tokens, width), BF16),
            jax.ShapeDtypeStruct((16, wide), F32),
        ),
        in_specs=[hbm] * 5,
        out_specs=(vmem, vmem, vmem),
        scratch_shapes=[
            V((model, width), BF16),
            V((16, model), BF16),
            V((2, NP, 16, wide), BF16),
            V((2, tokens, wide), BF16),
            V((2, tokens, width), BF16),
            V((2, NP, 16, width), BF16),
            *exchange(),
            *exchange(),
            V((NP, 16, wide), BF16),
            V((NP - 1, 16, wide), BF16),
            D((5,)), D((CHUNKS,)), D((NP - 1,)), D((NP,)), D((19,)), D((19,)), D((5,)), D((5,)),
        ],
        compiler_params=pltpu.CompilerParams(
            collective_id=0, has_side_effects=True, vmem_limit_bytes=56 * 2**20
        ),
        name="down_projection",
    )(hidden, down_weight, encoder.T, decoder.reshape(NP, 2, 16, wide), cotangent)

    return pl.pallas_call(
        write_out,
        out_shape=tuple(jax.ShapeDtypeStruct(r.shape, r.dtype) for r in results),
        in_specs=[vmem] * 3,
        out_specs=(hbm, hbm, hbm),
        scratch_shapes=[D((3,))],
        name="write_out",
    )(*results)


def solution(mesh):
    in_specs = (
        P("dp", "tensor"),
        P(None, "tensor"),
        P(None, "dp"),
        P(None, "tensor"),
        P("dp", "tensor"),
    )
    out_specs = (P("dp", "tensor"), P("dp", "tensor"), P("dp", "tensor"))
    return jax.shard_map(
        per_device, mesh=mesh, in_specs=in_specs, out_specs=out_specs, check_vma=False
    )
```

time: 538 us -> 63.2 us (0.12)
  waiting for transfers between devices: 418 us -> 0 us
  blocking collectives: 83 us -> 0 us
  Pallas kernels: 0 us -> 62.2 us
  matrix products: 20.6 us -> 0 us
  between operations: 13.8 us -> 0.64 us
    reduce_scatter x2 -> x0, waiting for transfers between devices: 212 us -> none  [the longest x1 134 us: per_device(): lax.psum_scatter(lax.dot_general(shared, cotangent, (((0,), (0,)), ((), (...]
    all_gather x1 -> x0, waiting for transfers between devices: 159 us -> none  [per_device(): full_code = lax.all_gather(encoder, 'dp', axis=1, tiled=True)]
    all_gather x2 -> x0, blocking collectives: 83 us -> none  [combine_latent(): return lax.all_gather(share, 'tensor', axis=1, tiled=True)]
    pallas_call x0 -> x2, Pallas kernels: none -> 62.2 us  [the longest x1 60.5 us: per_device(): pl.pallas_call(kernel, out_shape=(jax.ShapeDtypeStruct((tokens, wide), BF...]
    unnamed x5 -> x0, waiting for transfers between devices: 46.4 us -> none
    dot_general x4 -> x0, matrix products: 19.6 us -> none  [the longest x1 9.78 us: per_device(): jnp.dot(partial_value, full_code, preferred_element_type=jnp.float32)]
  transfers between devices with their start and end apart: 4 -> 0, of which waited for: 4 -> 0; matrix products, arithmetic and copies ran while one was open for 2% -> 0% of each run, Pallas kernels for 0% -> 0%
where the time goes in v1:
time: 63.2 us; the launch traced here: 62.8 us
  Pallas kernels  62.2 us (98%)
  between operations  0.64 us (1%)
    pallas_call x1, Pallas kernels, per_device(): pl.pallas_call(kernel, out_shape=(jax.ShapeDtypeStruct((tokens, wide), BF...  60.5 us
    pallas_call x1, Pallas kernels, per_device(): pl.pallas_call(write_out, out_shape=tuple((jax.ShapeDtypeStruct(r.shape,...  1.69 us

profile of v1, /device:TPU:6, one launch (start us, length us, event | category | flops | bytes accessed | tf_op | source)
XLA Modules:
  0.0 62.8 jit_solution(2172402201885702000)
XLA Ops:
  0.6 60.5 %down_projection.1 = (bf16[128,256]{1,0:T(8,128)(2,1)}, bf16[128,896]{1,0:T(8,128)(2,1)}, f32[16,256]{1,0:T(8,128)}) custom-call(bf16[128,896]{1,0:T(8,128)(2,1)} %h_hbm.1, bf16[4096,896]{1,0:T(8,128)(2,1)} %dw_hbm.1, bf16[16,4096]{1,0:T(8,128)(2,1)} %bitcast.3, bf16[24,2,16,256]{3,2,1,0:T(8,128)(2,1)} %bitcast.2, bf16[128,256]{1,0:T(8,128)(2,1)} %cot_hbm.1), custom_call_target="tpu_custom_call" | custom-call | tf_op jit(solution)/shard_map/down_projection/pallas_call | solution.py:286
  61.1 1.7 %write_out.1 = (bf16[128,256]{1,0:T(8,128)(2,1)}, bf16[128,896]{1,0:T(8,128)(2,1)}, f32[16,256]{1,0:T(8,128)}) custom-call(bf16[128,256]{1,0:T(8,128)(2,1)} %get-tuple-element.6.a, bf16[128,896]{1,0:T(8,128)(2,1)} %get-tuple-element.7.b, f32[16,256]{1,0:T(8,128)} %get-tuple-element.8.c), custom_call_target="tpu_custom_call" | custom-call | tf_op jit(solution)/shard_map/write_out/pallas_call | solution.py:314

commit v2 on v1

v2 whole, which is shorter than its diff:
```python
import jax
import jax.numpy as jnp
from jax import lax
from jax.experimental import pallas as pl
from jax.experimental.pallas import tpu as pltpu
from jax.sharding import PartitionSpec as P

MESH = pl.DeviceIdType.MESH
F32, BF16 = jnp.float32, jnp.bfloat16
NZ, NT = 12, 16
NP = 2 * NZ
PARTS = 3
STEP = NP // PARTS
CHUNKS = 8


def nt(a, b):
    return lax.dot_general(a, b, (((1,), (1,)), ((), ())), preferred_element_type=F32)


def nn(a, b):
    return jnp.dot(a, b, preferred_element_type=F32)


def tn(a, b):
    return lax.dot_general(a, b, (((0,), (0,)), ((), ())), preferred_element_type=F32)


def flat(x):
    return x.reshape(-1, x.shape[-1])


def kernel(
    h_hbm, dw_hbm, enc_hbm, dec_hbm, cot_hbm,
    out_hbm, gh_hbm, gd_hbm,
    dwv, encv, decv, cotv, hv, mv,
    gterm, gslot, gfull, gsib,
    sterm, sslot, sfull, ssib,
    dterm, dslot, outv, ghv, gdv,
    lsem, wsem, osem, msend, mrecv, psend, precv, asend, arecv,
):
    dp, t = lax.axis_index("dp"), lax.axis_index("tensor")
    z, yh, c = dp // 4, (dp // 2) % 2, dp % 2
    place = z * 2 + yh
    yo = 1 - yh

    def along(k):
        return lax.rem(z + (k + NZ) % NZ, NZ)

    def device(k, yy):
        return ((along(k) * 2 + yy) * 2 + c, t)

    sibling = (dp + 1 - 2 * c, t)

    depth = dw_hbm.shape[0] // CHUNKS
    own = [
        pltpu.make_async_copy(enc_hbm, encv, lsem.at[0]),
        pltpu.make_async_copy(cot_hbm, cotv.at[c], lsem.at[1]),
        pltpu.make_async_copy(h_hbm, hv.at[c], lsem.at[2]),
        pltpu.make_async_copy(dec_hbm.at[:, 0], decv.at[0], lsem.at[3]),
        pltpu.make_async_copy(dec_hbm.at[:, 1], decv.at[1], lsem.at[4]),
    ]
    weights = [
        pltpu.make_async_copy(
            dw_hbm.at[pl.ds(i * depth, depth)], dwv.at[pl.ds(i * depth, depth)], wsem.at[i]
        )
        for i in range(CHUNKS)
    ]
    own[0].start()
    for copy in weights:
        copy.start()
    for copy in own[1:]:
        copy.start()

    barrier = pltpu.get_barrier_semaphore()
    near = (1, -1, 2, -2)
    greet = [sibling, device(0, yo)]
    greet += [device(k, yh) for k in near]
    greet += [device(k, yh) for k in (4, -4)]
    for who in greet:
        pl.semaphore_signal(barrier, inc=1, device_id=who, device_id_type=MESH)

    @pl.loop(1, NT)
    def _(k):
        pl.semaphore_signal(
            barrier, inc=1, device_id=(dp, lax.rem(t + k, NT)), device_id_type=MESH
        )

    own[0].wait()
    code = jnp.zeros((16, dwv.shape[1]), F32)
    for i in range(CHUNKS):
        cut = pl.ds(i * depth, depth)
        weights[i].wait()
        code += nn(encv[:, cut], dwv[cut, :])
    mv[c, place] = code.astype(BF16)

    pl.semaphore_wait(barrier, len(greet) + NT - 1)

    sent = []

    def pass_on(slot, *to):
        for who in to:
            copy = pltpu.make_async_remote_copy(
                src_ref=mv.at[c, slot], dst_ref=mv.at[c, slot],
                send_sem=msend.at[len(sent)], recv_sem=mrecv.at[slot],
                device_id=who, device_id_type=MESH,
            )
            copy.start()
            sent.append(copy)

    def arrived(slot):
        pltpu.make_async_copy(mv.at[c, slot], mv.at[c, slot], mrecv.at[slot]).wait()

    pairs = []

    def to_sibling(src, dst):
        i = len(pairs)
        copy = pltpu.make_async_remote_copy(
            src_ref=src, dst_ref=dst, send_sem=psend.at[i], recv_sem=precv.at[i],
            device_id=sibling, device_id_type=MESH,
        )
        copy.start()
        pairs.append(copy)
        return copy

    def scatter(term, slots, i):
        @pl.loop(1, NT)
        def _(k):
            who = lax.rem(t + k, NT)
            pltpu.make_async_remote_copy(
                src_ref=term.at[who], dst_ref=slots.at[k - 1],
                send_sem=asend.at[i], recv_sem=arecv.at[i],
                device_id=(dp, who), device_id_type=MESH,
            ).start()

    def gather(full, i):
        @pl.loop(1, NT)
        def _(k):
            pltpu.make_async_remote_copy(
                src_ref=full.at[t], dst_ref=full.at[t],
                send_sem=asend.at[i], recv_sem=arecv.at[i],
                device_id=(dp, lax.rem(t + k, NT)), device_id_type=MESH,
            ).start()

    def all_of(ref, sem):
        pltpu.make_async_copy(ref, ref, sem).wait()

    def reduce(term, slots, full, i):
        all_of(slots, arecv.at[i])
        total = term[t].astype(F32)
        for k in range(NT - 1):
            total += slots[k].astype(F32)
        full[t] = total.astype(BF16)
        gather(full, i + 1)

    def split(term, value):
        rows = value.shape[0] // 8
        for s in range(2):
            for r in range(8):
                term[8 * s + r] = value[r * rows:(r + 1) * rows, s * 128:(s + 1) * 128].astype(BF16)

    up, down = device(4, yh), device(-4, yh)
    one, two = (device(1, yh), device(-1, yh)), (device(2, yh), device(-2, yh))
    pass_on(place, up, down, device(0, yo), *one, *two)

    for copy in own[1:]:
        copy.wait()
    cot_pair = to_sibling(cotv.at[c], cotv.at[c])
    hid_pair = to_sibling(hv.at[c], hv.at[c])

    cot_pair.wait_recv()
    split(gterm, nt(flat(decv[c]), flat(cotv[...])))
    scatter(gterm, gslot, 0)

    turn = jnp.where(z // 4 == 1, NZ - 4, 4)
    first, second = lax.rem(z + turn, NZ) * 2, lax.rem(z + NZ - turn, NZ) * 2
    arrived(first + yh)
    pass_on(first + yh, device(0, yo), *one)
    arrived(z * 2 + yo)
    pass_on(z * 2 + yo, *one, *two)
    arrived(second + yh)
    pass_on(second + yh, device(0, yo), *one)
    pass_on(along(-4) * 2 + yh, two[0])
    arrived(first + yo)
    pass_on(first + yo, *one)
    arrived(second + yo)
    pass_on(second + yo, *one)
    pass_on(along(4) * 2 + yo, two[1])

    hid_pair.wait_recv()
    hidden_both = flat(hv[...])
    m_pairs = []

    def latent(n):
        for r in range(STEP // 2):
            @pl.when(lax.rem(z, 4) != r)
            def _():
                arrived(n * STEP + 2 * r)
                arrived(n * STEP + 2 * r + 1)

        rows = pl.ds(n * STEP, STEP)
        m_pairs.append(to_sibling(mv.at[c, rows], mv.at[c, rows]))
        split(sterm.at[n], nt(flat(mv[c, rows]), hidden_both))
        scatter(sterm.at[n], sslot.at[n], 2 + 2 * n)

    s_pairs = []

    def shared(n):
        all_of(sfull.at[n, pl.ds(0, NT - 1)], arecv.at[3 + 2 * n])
        s_pairs.append(to_sibling(sfull.at[n, pl.ds(8 * (1 - c), 8)], ssib.at[n]))

    def decoder_terms(n):
        gd = nn(flat(sfull[n, 0:8]), cotv[0]) + nn(flat(sfull[n, 8:16]), cotv[1])
        dterm[n * STEP:(n + 1) * STEP] = gd.astype(BF16).reshape(STEP, 16, -1)

        @pl.loop(n * STEP, (n + 1) * STEP)
        def _(who):
            @pl.when(who != place)
            def _():
                pltpu.make_async_remote_copy(
                    src_ref=dterm.at[who], dst_ref=dslot.at[lax.rem(who - place + NP, NP) - 1],
                    send_sem=asend.at[8], recv_sem=arecv.at[8],
                    device_id=(who * 2 + c, t), device_id_type=MESH,
                ).start()

    reduce(gterm, gslot, gfull, 0)
    latent(0)
    latent(1)
    reduce(sterm.at[0], sslot.at[0], sfull.at[0], 2)
    latent(2)
    reduce(sterm.at[1], sslot.at[1], sfull.at[1], 4)
    all_of(gfull.at[pl.ds(0, NT - 1)], arecv.at[1])
    g_pair = to_sibling(gfull.at[pl.ds(8 * (1 - c), 8)], gsib)
    shared(0)
    decoder_terms(0)
    reduce(sterm.at[2], sslot.at[2], sfull.at[2], 6)
    shared(1)
    decoder_terms(1)

    for copy in m_pairs:
        copy.wait_recv()
    g_pair.wait_recv()
    gh = tn(flat(gfull[pl.ds(8 * c, 8)]), flat(mv[c]))
    gh += tn(flat(gsib[...]), flat(mv[1 - c]))
    ghv[...] = gh.astype(BF16)
    gh_out = pltpu.make_async_copy(ghv, gh_hbm, osem.at[0])
    gh_out.start()

    shared(2)
    decoder_terms(2)
    for copy in s_pairs:
        copy.wait_recv()
    value = tn(flat(sfull[:, pl.ds(8 * c, 8)]), flat(decv[c]))
    value += tn(flat(ssib[...]), flat(decv[1 - c]))
    outv[...] = value.astype(BF16)
    out_out = pltpu.make_async_copy(outv, out_hbm, osem.at[1])
    out_out.start()

    all_of(dslot, arecv.at[8])
    total = dterm[place].astype(F32)
    for k in range(NP - 1):
        total += dslot[k].astype(F32)
    gdv[...] = total * (1.0 / 6144.0**0.5)
    gd_out = pltpu.make_async_copy(gdv, gd_hbm, osem.at[2])
    gd_out.start()

    for copy in sent:
        copy.wait_send()
    for copy in pairs:
        copy.wait_send()
    for i, ref in enumerate((gslot, gslot) + (sslot.at[0],) * 6 + (dslot,)):
        all_of(ref, asend.at[i])
    gh_out.wait()
    out_out.wait()
    gd_out.wait()


def write_out(a, b, c, a_out, b_out, c_out, sem):
    copies = [
        pltpu.make_async_copy(src, dst, sem.at[i])
        for i, (src, dst) in enumerate(((a, a_out), (b, b_out), (c, c_out)))
    ]
    for copy in copies:
        copy.start()
    for copy in copies:
        copy.wait()


def per_device(hidden, down_weight, encoder, decoder, cotangent):
    tokens, width = hidden.shape
    model = down_weight.shape[0]
    wide = decoder.shape[1]
    hbm = pl.BlockSpec(memory_space=pltpu.HBM)
    V, D = pltpu.VMEM, pltpu.SemaphoreType.DMA
    out_shape = (
        jax.ShapeDtypeStruct((tokens, wide), BF16),
        jax.ShapeDtypeStruct((tokens, width), BF16),
        jax.ShapeDtypeStruct((16, wide), F32),
    )

    results = pl.pallas_call(
        kernel,
        out_shape=out_shape,
        in_specs=[hbm] * 5,
        out_specs=(hbm,) * 3,
        scratch_shapes=[
            V((model, width), BF16),
            V((16, model), BF16),
            V((2, NP, 16, wide), BF16),
            V((2, tokens, wide), BF16),
            V((2, tokens, width), BF16),
            V((2, NP, 16, width), BF16),
            V((NT, 16 * PARTS, 128), BF16),
            V((NT - 1, 16 * PARTS, 128), BF16),
            V((NT, 16 * PARTS, 128), BF16),
            V((NT // 2, 16 * PARTS, 128), BF16),
            V((PARTS, NT, 16, 128), BF16),
            V((PARTS, NT - 1, 16, 128), BF16),
            V((PARTS, NT, 16, 128), BF16),
            V((PARTS, NT // 2, 16, 128), BF16),
            V((NP, 16, wide), BF16),
            V((NP - 1, 16, wide), BF16),
            V((tokens, wide), BF16),
            V((tokens, width), BF16),
            V((16, wide), F32),
            D((5,)), D((CHUNKS,)), D((3,)), D((NP - 1,)), D((NP,)), D((9,)), D((9,)), D((9,)), D((9,)),
        ],
        compiler_params=pltpu.CompilerParams(
            collective_id=0, has_side_effects=True, vmem_limit_bytes=56 * 2**20
        ),
        name="down_projection",
    )(hidden, down_weight, encoder.T, decoder.reshape(NP, 2, 16, wide), cotangent)

    return pl.pallas_call(
        write_out,
        out_shape=out_shape,
        in_specs=[pl.BlockSpec(memory_space=pltpu.VMEM)] * 3,
        out_specs=(hbm,) * 3,
        scratch_shapes=[D((3,))],
        name="write_out",
    )(*results)


def solution(mesh):
    in_specs = (
        P("dp", "tensor"),
        P(None, "tensor"),
        P(None, "dp"),
        P(None, "tensor"),
        P("dp", "tensor"),
    )
    out_specs = (P("dp", "tensor"), P("dp", "tensor"), P("dp", "tensor"))
    return jax.shard_map(
        per_device, mesh=mesh, in_specs=in_specs, out_specs=out_specs, check_vma=False
    )
```

time: 63.2 us -> 55.9 us (0.88)
  Pallas kernels: 62.2 us -> 54.5 us
    pallas_call x2, Pallas kernels: 62.2 us -> 54.5 us  [the longest x1 52.8 us: per_device(): pl.pallas_call(kernel, out_shape=out_shape, in_specs=[hbm] * 5, out_specs...]
where the time goes in v2:
time: 55.9 us; the launch traced here: 55.2 us
  Pallas kernels  54.5 us (97%)
  between operations  0.64 us (1%)
    pallas_call x1, Pallas kernels, per_device(): pl.pallas_call(kernel, out_shape=out_shape, in_specs=[hbm] * 5, out_specs...  52.8 us
    pallas_call x1, Pallas kernels, per_device(): pl.pallas_call(write_out, out_shape=out_shape, in_specs=[pl.BlockSpec(mem...  1.69 us

profile of v2, /device:TPU:6, one launch (start us, length us, event | category | flops | bytes accessed | tf_op | source)
XLA Modules:
  0.0 55.2 jit_solution(1578850499780237108)
XLA Ops:
  0.6 52.8 %down_projection.1 = (bf16[128,256]{1,0:T(8,128)(2,1)}, bf16[128,896]{1,0:T(8,128)(2,1)}, f32[16,256]{1,0:T(8,128)}) custom-call(bf16[128,896]{1,0:T(8,128)(2,1)} %h_hbm.1, bf16[4096,896]{1,0:T(8,128)(2,1)} %dw_hbm.1, bf16[16,4096]{1,0:T(8,128)(2,1)} %bitcast.3, bf16[24,2,16,256]{3,2,1,0:T(8,128)(2,1)} %bitcast.2, bf16[128,256]{1,0:T(8,128)(2,1)} %cot_hbm.1), custom_call_target="tpu_custom_call" | custom-call | tf_op jit(solution)/shard_map/down_projection/pallas_call | solution.py:301
  53.5 1.7 %write_out.1 = (bf16[128,256]{1,0:T(8,128)(2,1)}, bf16[128,896]{1,0:T(8,128)(2,1)}, f32[16,256]{1,0:T(8,128)}) custom-call(bf16[128,256]{1,0:T(8,128)(2,1)} %get-tuple-element.6.a, bf16[128,896]{1,0:T(8,128)(2,1)} %get-tuple-element.7.b, f32[16,256]{1,0:T(8,128)} %get-tuple-element.8.c), custom_call_target="tpu_custom_call" | custom-call | tf_op jit(solution)/shard_map/write_out/pallas_call | solution.py:334

commit v3 on v2

--- a/solution.py
+++ b/solution.py
@@ -161,7 +161,7 @@
 
     up, down = device(4, yh), device(-4, yh)
     one, two = (device(1, yh), device(-1, yh)), (device(2, yh), device(-2, yh))
-    pass_on(place, up, down, device(0, yo), *one, *two)
+    pass_on(place, device(0, yo), up, down, *one, *two)
 
     for copy in own[1:]:
         copy.wait()

time: 55.9 us -> 55.9 us (level)
  no operation moved by 1% of the time
where the time goes in v3:
time: 55.9 us; the launch traced here: 55.2 us
  Pallas kernels  54.5 us (97%)
  between operations  0.64 us (1%)
    pallas_call x1, Pallas kernels, per_device(): pl.pallas_call(kernel, out_shape=out_shape, in_specs=[hbm] * 5, out_specs...  52.8 us
    pallas_call x1, Pallas kernels, per_device(): pl.pallas_call(write_out, out_shape=out_shape, in_specs=[pl.BlockSpec(mem...  1.69 us

profile of v3, /device:TPU:6, one launch (start us, length us, event | category | flops | bytes accessed | tf_op | source)
XLA Modules:
  0.0 55.2 jit_solution(15096304779356513895)
XLA Ops:
  0.6 52.8 %down_projection.1 = (bf16[128,256]{1,0:T(8,128)(2,1)}, bf16[128,896]{1,0:T(8,128)(2,1)}, f32[16,256]{1,0:T(8,128)}) custom-call(bf16[128,896]{1,0:T(8,128)(2,1)} %h_hbm.1, bf16[4096,896]{1,0:T(8,128)(2,1)} %dw_hbm.1, bf16[16,4096]{1,0:T(8,128)(2,1)} %bitcast.3, bf16[24,2,16,256]{3,2,1,0:T(8,128)(2,1)} %bitcast.2, bf16[128,256]{1,0:T(8,128)(2,1)} %cot_hbm.1), custom_call_target="tpu_custom_call" | custom-call | tf_op jit(solution)/shard_map/down_projection/pallas_call | solution.py:301
  53.5 1.7 %write_out.1 = (bf16[128,256]{1,0:T(8,128)(2,1)}, bf16[128,896]{1,0:T(8,128)(2,1)}, f32[16,256]{1,0:T(8,128)}) custom-call(bf16[128,256]{1,0:T(8,128)(2,1)} %get-tuple-element.6.a, bf16[128,896]{1,0:T(8,128)(2,1)} %get-tuple-element.7.b, f32[16,256]{1,0:T(8,128)} %get-tuple-element.8.c), custom_call_target="tpu_custom_call" | custom-call | tf_op jit(solution)/shard_map/write_out/pallas_call | solution.py:334
